TPU v7x, 128 devices: a whole 4x4x4 slice. The times are simulated.
128 devices in a mesh: lon: 16 (over z_hi, x, core), lat: 8 (over z_lo, y).
Axes of the slice: x: 4, y: 4, z: 4 (z_hi: 2, z_lo: 2; z = z_hi * 2 + z_lo), core: 2. Of those that a mesh axis runs over, the one named last changes fastest.
Arguments:
- fields: bfloat16 [2, 192, 384, 512], P(None, 'lat', 'lon'), may hold values from -6 to 6
- cotangent: bfloat16 [2, 192, 384, 512], P(None, 'lat', 'lon'), may hold values from -6 to 6
- qkv_weight: bfloat16 [512, 1536], replicated, may hold values from -1 to 1, as said below
- out_weight: bfloat16 [512, 512], replicated, may hold values from -0.25 to 0.25
Outputs:
- output_field: bfloat16 [2, 192, 384, 512], P(None, 'lat', 'lon')
- field_grad: bfloat16 [2, 192, 384, 512], P(None, 'lat', 'lon')
- qkv_grad: float32 [512, 1536], P(('lon', 'lat'))
- out_grad: float32 [512, 512], P(('lon', 'lat'))
Inputs may be any that keep to these rules, and one draw needn't show every extreme that they name: `qkv_weight`: a dense projection matrix, about 512^-0.5 in scale.
All inputs are finite; a program needn't handle non-finite values.
Results may differ from a plain program's by a relative error of at most 0.015.
Values may be sent and summed in bfloat16 or wider, within the bound.
A program may use at most 192 MiB of HBM per device.

v0:
```python
import jax
import jax.numpy as jnp
from jax import lax
from jax.sharding import PartitionSpec as P

HEADS = 16
WIN_LAT = 6
WIN_LON = 12


def from_behind(x, axis, by):
    length = lax.axis_size(axis)
    return lax.ppermute(x, axis, [(i, (i + by) % length) for i in range(length)])


def normalize(values):
    center = jnp.mean(values, axis=-1, keepdims=True)
    centred = values - center
    spread = jnp.mean(centred * centred, axis=-1, keepdims=True)
    return centred * lax.rsqrt(spread + 1e-05)


def attend(projected, groups):
    wincount, tokens_win, triple = projected.shape
    width = triple // 3
    head_size = width // HEADS
    queries = projected[..., :width].reshape(wincount, tokens_win, HEADS, head_size)
    keyset = projected[..., width : 2 * width].reshape(wincount, tokens_win, HEADS, head_size)
    valueset = projected[..., 2 * width :].reshape(wincount, tokens_win, HEADS, head_size)
    scores = jnp.einsum(
        "wqhe,wkhe->whqk", queries, keyset, preferred_element_type=jnp.float32
    ) * head_size ** (-0.5)
    allowed = (groups[:, :, None] == groups[:, None, :])[:, None]
    scores = jnp.where(allowed, scores, -1000000000.0)
    highest = jnp.max(scores, axis=-1, keepdims=True)
    raised = jnp.exp(scores - highest)
    soft_weights = (raised / jnp.sum(raised, axis=-1, keepdims=True)).astype(jnp.bfloat16)
    mixture = jnp.einsum(
        "whqk,wkhe->wqhe", soft_weights, valueset, preferred_element_type=jnp.float32
    )
    return mixture.reshape(wincount, tokens_win, width).astype(jnp.bfloat16)


def to_windows(grid):
    levels, lat_cells, lon_cells, channels = grid.shape
    shaped = grid.reshape(
        levels, lat_cells // WIN_LAT, WIN_LAT, lon_cells // WIN_LON, WIN_LON, channels
    )
    shaped = shaped.transpose(1, 3, 0, 2, 4, 5)
    return shaped.reshape(
        lat_cells // WIN_LAT * (lon_cells // WIN_LON), levels * WIN_LAT * WIN_LON, channels
    )


def from_windows(windows, levels, lat_cells, lon_cells):
    channels = windows.shape[-1]
    shaped = windows.reshape(
        lat_cells // WIN_LAT, lon_cells // WIN_LON, levels, WIN_LAT, WIN_LON, channels
    )
    shaped = shaped.transpose(2, 0, 3, 1, 4, 5)
    return shaped.reshape(levels, lat_cells, lon_cells, channels)


def roll_grid(field, direction):
    shift_lat = WIN_LAT // 2
    shift_lon = WIN_LON // 2
    cutoff = shift_lat if direction < 0 else field.shape[1] - shift_lat
    leading, trailing = (field[:, :cutoff], field[:, cutoff:])
    outgoing = leading if direction < 0 else trailing
    incoming = from_behind(outgoing, "lat", direction)
    field = jnp.concatenate([trailing, incoming] if direction < 0 else [incoming, leading], axis=1)
    cutoff = shift_lon if direction < 0 else field.shape[2] - shift_lon
    leading, trailing = (field[:, :, :cutoff], field[:, :, cutoff:])
    outgoing = leading if direction < 0 else trailing
    incoming = from_behind(outgoing, "lon", direction)
    return jnp.concatenate([trailing, incoming] if direction < 0 else [incoming, leading], axis=2)


def shards(fields, cotangent, qkv_weight, out_weight):
    levels, lat_cells, lon_cells, width = fields.shape
    rolled = roll_grid(fields, -1)
    windows = to_windows(rolled)
    wincount, tokens_win = (windows.shape[0], windows.shape[1])
    tokens_flat = windows.reshape(-1, width)
    lat_rows = lax.axis_index("lat") * lat_cells + jnp.arange(lat_cells, dtype=jnp.int32)
    group_rows = (lat_rows >= lat_cells * lax.axis_size("lat") - WIN_LAT // 2).astype(jnp.int32)
    group_grid = jnp.broadcast_to(
        group_rows[None, :, None, None], (levels, lat_cells, lon_cells, 1)
    )
    groups = to_windows(group_grid)[..., 0]
    norm_core, norm_back = jax.vjp(normalize, tokens_flat.astype(jnp.float32))
    normed = norm_core.astype(jnp.bfloat16)
    projected = jnp.dot(normed, qkv_weight, preferred_element_type=jnp.float32).astype(jnp.bfloat16)
    mixture, attend_back = jax.vjp(
        lambda values: attend(values, groups), projected.reshape(wincount, tokens_win, 3 * width)
    )
    attended = mixture.reshape(-1, width)
    output_rows = (
        tokens_flat.astype(jnp.float32)
        + jnp.dot(attended, out_weight, preferred_element_type=jnp.float32)
    ).astype(jnp.bfloat16)
    output_field = roll_grid(
        from_windows(
            output_rows.reshape(wincount, tokens_win, width), levels, lat_cells, lon_cells
        ),
        1,
    )
    grad_rows = to_windows(roll_grid(cotangent, -1)).reshape(-1, width)
    out_term = lax.dot_general(
        attended, grad_rows, (((0,), (0,)), ((), ())), preferred_element_type=jnp.float32
    )
    grad_attended = lax.dot_general(
        grad_rows, out_weight, (((1,), (1,)), ((), ())), preferred_element_type=jnp.float32
    ).astype(jnp.bfloat16)
    grad_projected = attend_back(grad_attended.reshape(wincount, tokens_win, width))[0].reshape(
        -1, 3 * width
    )
    qkv_term = lax.dot_general(
        normed, grad_projected, (((0,), (0,)), ((), ())), preferred_element_type=jnp.float32
    )
    grad_normed = lax.dot_general(
        grad_projected, qkv_weight, (((1,), (1,)), ((), ())), preferred_element_type=jnp.float32
    )
    grad_centred = norm_back(grad_normed)[0]
    grad_tokens = (grad_rows.astype(jnp.float32) + grad_centred).astype(jnp.bfloat16)
    field_grad = roll_grid(
        from_windows(
            grad_tokens.reshape(wincount, tokens_win, width), levels, lat_cells, lon_cells
        ),
        1,
    )
    qkv_grad, out_grad = (
        lax.psum_scatter(qkv_term, ("lon", "lat"), scatter_dimension=0, tiled=True),
        lax.psum_scatter(out_term, ("lon", "lat"), scatter_dimension=0, tiled=True),
    )
    return (output_field, field_grad, qkv_grad, out_grad)


def solution(mesh):
    placed = (P(None, "lat", "lon", None), P(None, "lat", "lon", None), P(), P())
    return jax.shard_map(
        shards,
        mesh=mesh,
        in_specs=placed,
        out_specs=(
            P(None, "lat", "lon", None),
            P(None, "lat", "lon", None),
            P(("lon", "lat"), None),
            P(("lon", "lat"), None),
        ),
        check_vma=False,
    )
```

profile of v0, /device:TPU:0, one launch (start us, length us, event | category | flops | bytes accessed | tf_op | source)
XLA Modules:
  0.0 403.0 jit_solution(3910975633792312276)
XLA Ops:
  8.3 4.5 %collective-permute-start.4 = (bf16[2,3,24,512]{3,2,1,0:T(8,128)(2,1)S(1)}, bf16[2,3,24,512]{3,2,1,0:T(8,128)(2,1)S(1)}, u32[]{:S(2)}, u32[]{:S(2)}) collective-permute-start(bf16[2,3,24,512]{3,2,1,0:T(8,128)(2,1)S(1)} %slice.69), channel_id=1, source_target_pairs={{0,7},{1,0},{2,1},{3,2},{4,3},{5,4},{6,5},{7,6},{8,15},{9,8},{10,9... | collective-permute-start | bytes 442376 | tf_op jit(solution)/shard_map/ppermute | solution.py:13
  20.0 4.1 %collective-permute-start.1 = (bf16[2,24,6,512]{3,2,1,0:T(8,128)(2,1)S(1)}, bf16[2,24,6,512]{3,2,1,0:T(8,128)(2,1)S(1)}, u32[]{:S(2)}, u32[]{:S(2)}) collective-permute-start(bf16[2,24,6,512]{3,2,1,0:T(8,128)(2,1)S(1)} %pad_maximum_fusion.4), channel_id=1, source_target_pairs={{0,120},{8,0},{16,8},{24,16},{32,24},{40,32},{48,40},{56,48},{64,5... | collective-permute-start | bytes 884744 | tf_op jit(solution)/shard_map/ppermute | solution.py:13
  37.1 3.9 multiply_reduce_fusion.1
  41.5 3.9 copy.71
  47.7 3.9 reshape.155
  63.4 3.8 reshape.149
  67.2 3.7 convolution_convert_fusion
  72.7 3.5 copy.79
  82.5 12.4 %fusion.5 = (f32[8,16,144]{2,1,0:T(8,128)S(1)}, f32[8,16,144,144]{2,3,1,0:T(8,128)}) fusion(pred[8,144,144]{1,2,0:T(8,128)(4,1)S(1)} %broadcast_compare_fusion, bf16[8,144,16,32]{1,3,2,0:T(8,128)(2,1)} %bitcast.58, bf16[8,144,16,32]{1,3,2,0:T(8,128)(2,1)} %bitcast.60), kind=kOutput, calls=%fused_computation.12 | convolution fusion | flops 177813504 | bytes 13215744 | tf_op jit(solution)/shard_map/jvp(wqhe,wkhe->whqk)/dot_general | solution.py:30
  94.9 11.7 %fusion.16 = f32[8,16,144]{2,1,0:T(8,128)S(1)} fusion(f32[8,16,144]{2,1,0:T(8,128)S(1)} %get-tuple-element.31, f32[8,16,144,144]{2,3,1,0:T(8,128)} %get-tuple-element.32, pred[8,144,144]{1,2,0:T(8,128)(4,1)S(1)} %broadcast_compare_fusion), kind=kLoop, calls=%fused_computation.25 | loop fusion | flops 10598400 | bytes 10930176 | tf_op jit(solution)/shard_map/jvp()/reduce_sum | solution.py:37
  106.7 21.5 %convert_reduce_fusion = (f32[8,16,144]{2,1,0:T(8,128)}, pred[8,16,144,144]{2,3,1,0:T(8,128)(4,1)}, f32[8,16,144]{2,1,0:T(8,128)S(1)}, bf16[8,16,144,144]{2,3,1,0:T(8,128)(2,1)}) fusion(f32[8,16,144]{2,1,0:T(8,128)S(1)} %get-tuple-element.31, f32[8,16,144,144]{2,3,1,0:T(8,128)} %get-tuple-element.32, pred[8,144,144]{1,2,0:T(8,128)(4,1)S(1)} %broadcast_compare_fusion, ...), kind=kOutput, calls=%fused_computation.7 | convolution fusion | flops 199028736 | bytes 21399552 | tf_op jit(solution)/shard_map/transpose(jvp(whqk,wkhe->wqhe))/dot_general | solution.py:38
  128.3 20.4 %fusion.33 = (f32[8,16,144]{2,1,0:T(8,128)S(1)}, f32[8,16,144,144]{2,3,1,0:T(8,128)}, bf16[8,16,144,144]{2,3,1,0:T(8,128)(2,1)S(1)}) fusion(f32[8,16,144]{2,1,0:T(8,128)} %copy-done.7, f32[8,16,144,144]{2,3,1,0:T(8,128)} %get-tuple-element.32, pred[8,144,144]{1,2,0:T(8,128)(4,1)} %copy-done.6, f32[8,16,144]{2,1,0:T(8,128)S(1)} %neg.12, ...), kind=kLoop, calls=%fused_computation.73 | loop fusion | flops 26523648 | bytes 32311296 | tf_op jit(solution)/shard_map/transpose(jvp())/reduce_sum | solution.py:36
  149.4 14.4 %fusion.19 = bf16[8,16,144,32]{2,3,1,0:T(8,128)(2,1)} fusion(bf16[8,144,16,32]{1,3,2,0:T(8,128)(2,1)} %bitcast.61, f32[8,16,144,144]{2,3,1,0:T(8,128)} %get-tuple-element.21, pred[8,16,144,144]{2,3,1,0:T(8,128)(4,1)} %get-tuple-element.23, f32[8,16,144]{2,1,0:T(8,128)} %negate_divide_fusion, pred[8,144,144]{1,2,0:T(8,128)(4,1)} %copy-done.6), kind=kOutput, calls=%fused_computation.38 | convolution fusion | flops 181075968 | bytes 15869952 | tf_op jit(solution)/shard_map/transpose(jvp(wqhe,wkhe->whqk))/dot_general | solution.py:30
  163.8 12.6 %fusion.18 = bf16[8,16,144,32]{2,3,1,0:T(8,128)(2,1)} fusion(bf16[8,144,16,32]{1,3,2,0:T(8,128)(2,1)} %bitcast.59, f32[8,16,144,144]{2,3,1,0:T(8,128)} %get-tuple-element.21, pred[8,16,144,144]{2,3,1,0:T(8,128)(4,1)} %get-tuple-element.23, f32[8,16,144]{2,1,0:T(8,128)} %negate_divide_fusion, pred[8,144,144]{1,2,0:T(8,128)(4,1)} %copy-done.6), kind=kOutput, calls=%fused_computation.37 | convolution fusion | flops 181075968 | bytes 15869952 | tf_op jit(solution)/shard_map/transpose(jvp(wqhe,wkhe->whqk))/dot_general | solution.py:30
  176.4 6.0 %convolution_convert_fusion.3 = bf16[8,16,32,144]{3,2,1,0:T(8,128)(2,1)} fusion(bf16[8,16,144,144]{2,3,1,0:T(8,128)(2,1)S(1)} %get-tuple-element.24, bf16[8,16,32,144]{3,0,2,1:T(8,128)(2,1)} %bitcast.63), kind=kOutput, calls=%fused_computation.39 | convolution fusion | flops 170459136 | bytes 7667712 | tf_op jit(solution)/shard_map/transpose(jvp(whqk,wkhe->wqhe))/dot_general | solution.py:38
  188.0 3.7 convert_element_type.104
  212.7 3.7 copy.91
  216.3 3.9 copy.93
  220.2 3.7 copy.88
  226.6 3.6 multiply_reduce_fusion
  230.2 3.9 fusion.37
  249.4 5.9 %collective-permute-done.6 = bf16[2,3,24,512]{3,0,2,1:T(2,128)(2,1)S(1)} collective-permute-done((bf16[2,3,24,512]{3,0,2,1:T(2,128)(2,1)}, bf16[2,3,24,512]{3,0,2,1:T(2,128)(2,1)S(1)}, u32[]{:S(2)}, u32[]{:S(2)}) %collective-permute-start.6) | collective-permute-done | bytes 147488 | tf_op jit(solution)/shard_map/ppermute | solution.py:13
  258.6 8.5 %collective-permute-done.7 = bf16[2,24,6,512]{3,0,2,1:T(2,128)(2,1)S(1)} collective-permute-done((bf16[2,24,6,512]{3,0,2,1:T(2,128)(2,1)S(1)}, bf16[2,24,6,512]{3,0,2,1:T(2,128)(2,1)S(1)}, u32[]{:S(2)}, u32[]{:S(2)}) %collective-permute-start.7) | collective-permute-done | bytes 294944 | tf_op jit(solution)/shard_map/ppermute | solution.py:13
  270.0 123.1 %all-reduce.8.cloned.1.call-done = (f32[512,1536]{1,0:T(8,128)}, f32[512,512]{1,0:T(8,128)}) async-done(((f32[512,1536]{1,0:T(8,128)}, f32[512,512]{1,0:T(8,128)}), (f32[512,1536]{1,0:T(8,128)}, f32[512,512]{1,0:T(8,128)})) %all-reduce.8.cloned.1.call-update) | async-done | bytes 4194320
  (108 shorter events, 97.9 us)
Async XLA Ops:
  7.2 60.0 %copy-start = (bf16[512,1536]{1,0:T(8,128)(2,1)S(1)}, bf16[512,1536]{1,0:T(8,128)(2,1)}, u32[]{:S(2)}) copy-start(bf16[512,1536]{1,0:T(8,128)(2,1)} %param.6) | copy-start | bytes 4718596
  7.2 9.8 %copy-start.9 = (bf16[2,24,24,512]{3,2,1,0:T(8,128)(2,1)S(1)}, bf16[2,24,24,512]{3,2,1,0:T(8,128)(2,1)}, u32[]{:S(2)}) copy-start(bf16[2,24,24,512]{3,2,1,0:T(8,128)(2,1)} %param.5) | copy-start | bytes 3538948
  7.2 386.0 %all-reduce.8.cloned.1.call-start = ((), (), s32[]{:S(2)}) async-start(), calls=%async_computation | async-start | bytes 8388608
  8.3 15.7 %collective-permute-start.4 = (bf16[2,3,24,512]{3,2,1,0:T(8,128)(2,1)S(1)}, bf16[2,3,24,512]{3,2,1,0:T(8,128)(2,1)S(1)}, u32[]{:S(2)}, u32[]{:S(2)}) collective-permute-start(bf16[2,3,24,512]{3,2,1,0:T(8,128)(2,1)S(1)} %slice.69), channel_id=1, source_target_pairs={{0,7},{1,0},{2,1},{3,2},{4,3},{5,4},{6,5},{7,6},{8,15},{9,8},{10,9... | collective-permute-start | bytes 442376 | tf_op jit(solution)/shard_map/ppermute | solution.py:13
  14.4 5.5 %collective-permute-start = (bf16[2,3,24,512]{3,2,1,0:T(8,128)(2,1)}, bf16[2,3,24,512]{3,2,1,0:T(8,128)(2,1)S(1)}, u32[]{:S(2)}, u32[]{:S(2)}) collective-permute-start(bf16[2,3,24,512]{3,2,1,0:T(8,128)(2,1)} %slice.58), channel_id=1, source_target_pairs={{0,7},{1,0},{2,1},{3,2},{4,3},{5,4},{6,5},{7,6},{8,15},{9,8},{10,9... | collective-permute-start | bytes 442376 | tf_op jit(solution)/shard_map/ppermute | solution.py:13
  15.6 91.1 %copy-start.6 = (pred[8,144,144]{1,2,0:T(8,128)(4,1)}, pred[8,144,144]{1,2,0:T(8,128)(4,1)S(1)}, u32[]{:S(2)}) copy-start(pred[8,144,144]{1,2,0:T(8,128)(4,1)S(1)} %broadcast_compare_fusion) | copy-start | bytes 497668
  20.0 9.4 %collective-permute-start.1 = (bf16[2,24,6,512]{3,2,1,0:T(8,128)(2,1)S(1)}, bf16[2,24,6,512]{3,2,1,0:T(8,128)(2,1)S(1)}, u32[]{:S(2)}, u32[]{:S(2)}) collective-permute-start(bf16[2,24,6,512]{3,2,1,0:T(8,128)(2,1)S(1)} %pad_maximum_fusion.4), channel_id=1, source_target_pairs={{0,120},{8,0},{16,8},{24,16},{32,24},{40,32},{48,40},{56,48},{64,5... | collective-permute-start | bytes 884744 | tf_op jit(solution)/shard_map/ppermute | solution.py:13
  24.8 26.8 %collective-permute-start.5 = (bf16[2,24,6,512]{3,2,1,0:T(8,128)(2,1)}, bf16[2,24,6,512]{3,2,1,0:T(8,128)(2,1)}, u32[]{:S(2)}, u32[]{:S(2)}) collective-permute-start(bf16[2,24,6,512]{3,2,1,0:T(8,128)(2,1)} %pad_maximum_fusion.3), channel_id=1, source_target_pairs={{0,120},{8,0},{16,8},{24,16},{32,24},{40,32},{48,40},{56,48},{64,5... | collective-permute-start | bytes 884744 | tf_op jit(solution)/shard_map/ppermute | solution.py:13
  57.8 1.0 copy-start.4
  94.9 11.8 %copy-start.7 = (f32[8,16,144]{2,1,0:T(8,128)}, f32[8,16,144]{2,1,0:T(8,128)S(1)}, u32[]{:S(2)}) copy-start(f32[8,16,144]{2,1,0:T(8,128)S(1)} %get-tuple-element.31) | copy-start | bytes 221188
  106.7 21.6 %copy-start.8 = (f32[8,16,144]{2,1,0:T(8,128)}, f32[8,16,144]{2,1,0:T(8,128)S(1)}, u32[]{:S(2)}) copy-start(f32[8,16,144]{2,1,0:T(8,128)S(1)} %fusion.16) | copy-start | bytes 221188
  128.3 20.4 %copy-start.14 = (f32[8,16,144]{2,1,0:T(8,128)S(1)}, f32[8,16,144]{2,1,0:T(8,128)}, u32[]{:S(2)}) copy-start(f32[8,16,144]{2,1,0:T(8,128)} %get-tuple-element.22) | copy-start | bytes 221188
  191.7 3.3 copy-start.1
  191.7 3.3 copy-start.11
  200.0 4.3 %copy-start.12 = (f32[4,2,2,6,12]{4,0,3,2,1:T(4,128)S(1)}, f32[4,2,2,6,12]{4,0,3,2,1:T(4,128)}, u32[]{:S(2)}) copy-start(f32[4,2,2,6,12]{4,0,3,2,1:T(4,128)} %get-tuple-element.29) | copy-start | bytes 13828
  220.2 3.7 copy-start.13
  223.9 2.7 copy-start.2
  223.9 13.5 %collective-permute-start.2 = (bf16[2,3,24,512]{3,0,2,1:T(2,128)(2,1)S(1)}, bf16[2,3,24,512]{3,0,2,1:T(2,128)(2,1)S(1)}, u32[]{:S(2)}, u32[]{:S(2)}) collective-permute-start(bf16[2,3,24,512]{3,0,2,1:T(2,128)(2,1)S(1)} %copy-done.13), channel_id=1, source_target_pairs={{0,1},{1,2},{2,3},{3,4},{4,5},{5,6},{6,7},{7,0},{8,9},{9,10},{10,1... | collective-permute-start | bytes 442376 | tf_op jit(solution)/shard_map/ppermute | solution.py:13
  226.6 3.6 copy-start.10
  234.2 3.7 copy-start.5
  237.8 17.9 %collective-permute-start.3 = (bf16[2,24,6,512]{3,0,2,1:T(2,128)(2,1)S(1)}, bf16[2,24,6,512]{3,0,2,1:T(2,128)(2,1)S(1)}, u32[]{:S(2)}, u32[]{:S(2)}) collective-permute-start(bf16[2,24,6,512]{3,0,2,1:T(2,128)(2,1)S(1)} %pad_maximum_fusion.6), channel_id=1, source_target_pairs={{0,8},{8,16},{16,24},{24,32},{32,40},{40,48},{48,56},{56,64},{64,7... | collective-permute-start | bytes 884744 | tf_op jit(solution)/shard_map/ppermute | solution.py:13
  245.0 1.0 copy-start.3
  246.8 8.4 %collective-permute-start.6 = (bf16[2,3,24,512]{3,0,2,1:T(2,128)(2,1)}, bf16[2,3,24,512]{3,0,2,1:T(2,128)(2,1)S(1)}, u32[]{:S(2)}, u32[]{:S(2)}) collective-permute-start(bf16[2,3,24,512]{3,0,2,1:T(2,128)(2,1)} %slice.85), channel_id=1, source_target_pairs={{0,1},{1,2},{2,3},{3,4},{4,5},{5,6},{6,7},{7,0},{8,9},{9,10},{10,1... | collective-permute-start | bytes 442376 | tf_op jit(solution)/shard_map/ppermute | solution.py:13
  255.6 11.5 %collective-permute-start.7 = (bf16[2,24,6,512]{3,0,2,1:T(2,128)(2,1)S(1)}, bf16[2,24,6,512]{3,0,2,1:T(2,128)(2,1)S(1)}, u32[]{:S(2)}, u32[]{:S(2)}) collective-permute-start(bf16[2,24,6,512]{3,0,2,1:T(2,128)(2,1)S(1)} %pad_maximum_fusion.5), channel_id=1, source_target_pairs={{0,8},{8,16},{16,24},{24,32},{32,40},{40,48},{48,56},{56,64},{64,7... | collective-permute-start | bytes 884744 | tf_op jit(solution)/shard_map/ppermute | solution.py:13
Sparse Core Ops, SparseCore 0:
  234.3 158.8 all-reduce.7
where the time goes:
time: 410 us; the launch traced here: 403 us
  waiting for transfers between devices  142 us (35%)
  matrix products  89 us (22%)
  local copies, waits for them, and re-layouts  85.8 us (21%)
  other arithmetic  59.1 us (14%)
  between operations  14.7 us (4%)
  starting transfers between devices  11.9 us (3%)
    unnamed x2, waiting for transfers between devices  123 us
    dot_general x3, matrix products, attend(): jnp.einsum('wqhe,wkhe->whqk', queries, keyset, preferred_element_type=jnp...  39.4 us
    dot_general x3, matrix products, attend(): jnp.einsum('whqk,wkhe->wqhe', soft_weights, valueset, preferred_element_t...  30.4 us
    reduce_sum x1, other arithmetic, attend(): raised = jnp.exp(scores - highest)  20.4 us
    ppermute x8, waiting for transfers between devices, from_behind(): lax.ppermute(x, axis, [(i, (i + by) % length) for i in range(length)])  19.3 us
    ppermute x8, starting transfers between devices, from_behind(): lax.ppermute(x, axis, [(i, (i + by) % length) for i in range(length)])  11.8 us
    reduce_sum x1, other arithmetic, attend(): jnp.sum(raised, axis=-1, keepdims=True)  11.7 us
    convert_element_type x3, local copies, waits for them, and re-layouts, shards(): tokens_flat.astype(jnp.float32)  11 us
  transfers between devices with their start and end apart: 9, of which 5 were waited for; matrix products, arithmetic and copies ran while one was open for 14% of the time, Pallas kernels for 0%

commit v1 on v0

v1 whole, which is shorter than its diff:
```python
import functools, math
import jax
import jax.numpy as jnp
from jax import lax
from jax.experimental import pallas as pl
from jax.experimental.pallas import tpu as pltpu
from jax.sharding import PartitionSpec as P

D = 512
HEADS = 16
HD = 32
T = 144
NW = 8
TOK = NW * T
F32 = jnp.float32
BF = jnp.bfloat16
EPS = 1e-5
SCALE = HD ** -0.5
LOG2E = math.log2(math.e)
LN2 = math.log(2.0)


def nt(a, b):
    return lax.dot_general(a, b, (((1,), (1,)), ((), ())), preferred_element_type=F32)


def nn(a, b):
    return lax.dot_general(a, b, (((1,), (0,)), ((), ())), preferred_element_type=F32)


def tn(a, b):
    return lax.dot_general(a, b, (((0,), (0,)), ((), ())), preferred_element_type=F32)


def norm_stats(x):
    mean = jnp.sum(x, axis=-1, keepdims=True) * (1.0 / D)
    xc = x - mean
    var = jnp.sum(xc * xc, axis=-1, keepdims=True) * (1.0 / D)
    return xc, lax.rsqrt(var + EPS)


def heads_apart(a):
    lane = lax.broadcasted_iota(jnp.int32, (1, 128), 1) // HD
    zero = jnp.zeros((T, 128), BF)
    parts = []
    for h in range(8):
        mask = jnp.where(lane == h % 4, 1.0, 0.0).astype(BF)
        own = a[:, 128 * (h // 4) : 128 * (h // 4) + 128] * mask
        parts.append(jnp.concatenate([own, zero] if h < 4 else [zero, own], axis=1))
    return jnp.concatenate(parts, axis=0)


def heads_together(a):
    lane = lax.broadcasted_iota(jnp.int32, (1, 128), 1) // HD
    halves = []
    for c in range(2):
        cols = slice(128 * c, 128 * c + 128)
        own = a[T * 4 * c : T * 4 * c + T, cols]
        for h in range(1, 4):
            at = T * (4 * c + h)
            own = jnp.where(lane == h, a[at : at + T, cols], own)
        halves.append(own)
    return jnp.concatenate(halves, axis=1)


def attention(w, big, q_s, k_s, v_s, do_s, o_s, dp_s):
    rows = pl.ds(pl.multiple_of(w * T, 16), T)
    half = T // 2
    query = lax.broadcasted_iota(jnp.int32, (1, 8 * T), 1) % T
    pen0 = jnp.where(query >= half, big, 0.0)
    pen1 = jnp.where(query < half, big, 0.0)
    for g in range(2):
        qg = q_s[g, rows, :]
        kg = k_s[g, rows, :]
        vg = v_s[g, rows, :]
        qm = heads_apart(qg)
        dom = heads_apart(do_s[g, rows, :])
        st = nt(kg, qm)
        dpt = nt(vg, dom)
        top = jnp.maximum(
            jnp.max(st[:half], axis=0, keepdims=True) - pen0, jnp.max(st[half:], axis=0, keepdims=True) - pen1
        )
        e = jnp.concatenate([jnp.exp2(st[:half] - (top + pen0)), jnp.exp2(st[half:] - (top + pen1))], axis=0)
        p = e * (1.0 / jnp.sum(e, axis=0, keepdims=True))
        pb = p.astype(BF)
        ds = (p * (dpt - jnp.sum(p * dpt, axis=0, keepdims=True))).astype(BF)
        cols = slice(256 * g, 256 * g + 256)
        o_s[rows, cols] = heads_together(tn(pb, vg)).astype(BF)
        dp_s[rows, 1024 + 256 * g : 1280 + 256 * g] = nn(pb, dom).astype(BF)
        dp_s[rows, 512 + 256 * g : 768 + 256 * g] = (nn(ds, qm) * LN2).astype(BF)
        dp_s[rows, cols] = (heads_together(tn(ds, kg)) * SCALE).astype(BF)


MESH = pl.DeviceIdType.MESH
E_AT, S_AT, C_AT, MSG = 0, 256, 368, 416
PARTS = ((E_AT, 256), (S_AT, 112), (C_AT, 48))
FREE = 3 * T


def window_of(i, j):
    if i < 3:
        return i + 3 * j
    return 6 + j


def neighbours(by):
    lon, lat = lax.axis_index("lon"), lax.axis_index("lat")
    nlon, nlat = lax.axis_size("lon"), lax.axis_size("lat")
    lon2, lat2 = lax.rem(lon + by + nlon, nlon), lax.rem(lat + by + nlat, nlat)
    return [(lon2, lat), (lon, lat2), (lon2, lat2)]


def halo_copies(which, send, recv, send_sem, recv_sem, to):
    return [
        pltpu.make_async_remote_copy(
            src_ref=send.at[which, pl.ds(at, rows)],
            dst_ref=recv.at[which, pl.ds(at, rows)],
            send_sem=send_sem.at[which, n],
            recv_sem=recv_sem.at[which, n],
            device_id=peer,
            device_id_type=MESH,
        )
        for n, ((at, rows), peer) in enumerate(zip(PARTS, to))
    ]


def kernel(
    f_ref, c_ref, w_ref, wo_ref, of_ref, df_ref, qg_ref, og_ref,
    wide, rows_s, pack, send_in, recv_in, send_out, recv_out, in_send, in_recv, out_send, out_recv,
    xw, gw, xn_s, q_s, k_s, v_s, do_s, o_s, dp_s, wt_s, wot_s,
    wg, r0, t0, r1x, r1z, t1x, t1z, r2, tc, t3f, t3, r3, rs_send, rs_recv,
):
    lon, lat = lax.axis_index("lon"), lax.axis_index("lat")
    core, x, zh = lax.rem(lon, 2), lax.rem(lon // 2, 4), lon // 8
    y, zl = lax.rem(lat, 4), lat // 4
    z = zh * 2 + zl

    def at(zh_, x_, core_, zl_, y_):
        return ((zh_ * 4 + x_) * 2 + core_, zl_ * 4 + y_)

    def step(v, d):
        return lax.rem(v + d, 4)

    partner = at(zh, x, 1 - core, zl, y)
    along_x = [at(zh, step(x, d), core, zl, y) for d in (1, 2, 3)]
    along_z = [at(step(z, d) // 2, x, core, lax.rem(step(z, d), 2), y) for d in (1, 2, 3)]
    along_y = [at(zh, x, core, zl, step(y, d)) for d in (1, 2, 3)]
    ahead, behind = neighbours(1), neighbours(-1)
    peers = ahead + behind + [partner] + along_x + along_z + along_y
    barrier = pltpu.get_barrier_semaphore()
    for peer in peers:
        pl.semaphore_signal(barrier, inc=1, device_id=peer, device_id_type=MESH)

    def rdma(src, dst, n, peer):
        copy = pltpu.make_async_remote_copy(
            src_ref=src, dst_ref=dst, send_sem=rs_send.at[n], recv_sem=rs_recv.at[n],
            device_id=peer, device_id_type=MESH,
        )
        copy.start()
        return copy

    halo_in = []
    for which, src in enumerate((f_ref, c_ref)):
        for l in range(2):
            for a in range(24):
                i, ar = (a - 3) // 6, (a - 3) % 6
                if a < 3:
                    row = src[l, a].astype(F32)
                    n = l * 3 + a
                    pack[S_AT + n * 12 : S_AT + n * 12 + 12] = row[6:18]
                    pack[S_AT + 72 + n * 6 : S_AT + 72 + n * 6 + 6] = row[18:24]
                    pack[C_AT + n * 6 : C_AT + n * 6 + 6] = row[0:6]
                else:
                    row = src[l, a, 0:16].astype(F32)
                    n = l * 6 + ar if i < 3 else l * 3 + ar
                    pack[E_AT + 72 * i + n * 6 : E_AT + 72 * i + n * 6 + 6] = row[0:6]
        send_in[which] = pack[...].astype(BF)
        if which == 0:
            pl.semaphore_wait(barrier, len(peers))
        halo_in.append(halo_copies(which, send_in, recv_in, in_send, in_recv, behind))
        for copy in halo_in[-1]:
            copy.start()

    for which, src in enumerate((f_ref, c_ref)):
        for l in range(2):
            for a in range(3, 24):
                i, ar = (a - 3) // 6, (a - 3) % 6
                row = src[l, a].astype(F32)
                n = l * 6 + ar if i < 3 else l * 3 + ar
                wide[which, window_of(i, 0), n * 12 : n * 12 + 12] = row[6:18]
                wide[which, window_of(i, 1), n * 6 : n * 6 + 6] = row[18:24]
    wt_s[...] = w_ref[...].T
    wot_s[...] = wo_ref[...].T

    def project(first, count):
        rows = slice(first * T, (first + count) * T)
        for w in range(first, first + count):
            at_ = slice(w * T, w * T + T)
            gw[at_] = wide[1, w].astype(BF)
            xv = wide[0, w]
            xw[at_] = xv.astype(BF)
            xc, rstd = norm_stats(xv)
            xn_s[at_] = (xc * rstd).astype(BF)
        for part, (dst, scale) in enumerate(((q_s, SCALE * LOG2E), (k_s, None), (v_s, None))):
            for n in range(2):
                res = nn(xn_s[rows], w_ref[:, 512 * part + 256 * n : 512 * part + 256 * n + 256])
                if scale is not None:
                    res = res * scale
                dst[n, rows] = res.astype(BF)
        for n in range(2):
            do_s[n, rows] = nn(gw[rows], wot_s[:, 256 * n : 256 * n + 256]).astype(BF)

    last = jnp.where(lat == lax.axis_size("lat") - 1, 1e9, 0.0)

    def attend(first, count):
        def window(w, _):
            big = jnp.where(w >= NW - 2, last, 0.0).astype(F32)
            attention(w, big, q_s, k_s, v_s, do_s, o_s, dp_s)
            return 0

        lax.fori_loop(first, first + count, window, 0)

    def finish_out(first, count):
        for w in range(first, first + count):
            at_ = slice(w * T, w * T + T)
            wide[0, w] = xw[at_].astype(F32) + nn(o_s[at_], wo_ref[...])

    def finish_grad(first, count):
        for w in range(first, first + count):
            at_ = slice(w * T, w * T + T)
            gn = nn(dp_s[at_], wt_s[...])
            xc, rstd = norm_stats(xw[at_].astype(F32))
            xh = xc * rstd
            m1 = jnp.sum(gn, axis=-1, keepdims=True) * (1.0 / D)
            m2 = jnp.sum(gn * xh, axis=-1, keepdims=True) * (1.0 / D)
            wide[1, w] = gw[at_].astype(F32) + rstd * (gn - m1 - xh * m2)

    project(0, 3)
    attend(0, 1)

    for which in range(2):
        for copy in halo_in[which]:
            copy.wait()
        pack[...] = recv_in[which].astype(F32)
        for i in range(3):
            wide[which, 3 + i, 72:144] = pack[E_AT + 72 * i : E_AT + 72 * i + 72]
        wide[which, 7, 36:72] = pack[E_AT + 216 : E_AT + 252]
        wide[which, 6, 72:144] = pack[S_AT : S_AT + 72]
        wide[which, 7, 72:108] = pack[S_AT + 72 : S_AT + 108]
        wide[which, 7, 108:144] = pack[C_AT : C_AT + 36]

    project(3, 5)
    attend(3, 5)

    halo_out = []
    for which, finish in enumerate((finish_out, finish_grad)):
        finish(3, 5)
        for i in range(3):
            pack[E_AT + 72 * i : E_AT + 72 * i + 72] = wide[which, 3 + i, 72:144]
        pack[E_AT + 216 : E_AT + 252] = wide[which, 7, 36:72]
        pack[S_AT : S_AT + 72] = wide[which, 6, 72:144]
        pack[S_AT + 72 : S_AT + 108] = wide[which, 7, 72:108]
        pack[C_AT : C_AT + 36] = wide[which, 7, 108:144]
        send_out[which] = pack[...].astype(BF)
        halo_out.append(halo_copies(which, send_out, recv_out, out_send, out_recv, ahead))
        for copy in halo_out[-1]:
            copy.start()

    attend(1, 2)

    def term(b):
        if b < 3:
            res = tn(xn_s[...], dp_s[:, 512 * b : 512 * b + 512])
        else:
            res = tn(o_s[...], gw[...])
        wg[b] = res.astype(BF).reshape(2, 4, 2, 2, 16, 512)
        return rdma(wg.at[b, :, :, 1 - core], r0.at[b], b, partner)

    def first_axis(b):
        copies = []
        for a in range(2):
            for k in range(4):
                t0[b, a, k] = (wg[b, a, k, core].astype(F32) + r0[b, a, k].astype(F32)).astype(BF)
        for d in (1, 2, 3):
            xd, zd = step(x, d), step(z, d)
            if b % 2 == 0:
                src, to = t0.at[b, :, xd], along_x[d - 1]
            else:
                src, to = t0.at[b, zd // 2, :, lax.rem(zd, 2)], along_z[d - 1]
            dst = (r1z if b % 2 else r1x).at[b // 2, d - 1]
            copies.append(rdma(src, dst, 4 + 3 * b + d - 1, to))
        return copies

    core_copies = [term(0), term(1)]
    stage1 = []
    core_copies[0].wait()
    stage1.append(first_axis(0))
    core_copies.append(term(2))
    core_copies[1].wait()
    stage1.append(first_axis(1))
    core_copies.append(term(3))
    core_copies[2].wait()
    stage1.append(first_axis(2))
    finish_out(0, 3)
    core_copies[3].wait()
    stage1.append(first_axis(3))
    finish_grad(0, 3)

    def second_axis(b):
        for copy in stage1[b]:
            copy.wait()
        copies = []
        got, t1 = (r1z, t1z) if b % 2 else (r1x, t1x)
        if b % 2 == 0:
            acc = t0[b, :, x].astype(F32)
        else:
            acc = t0[b, zh, :, zl].astype(F32)
        for d in range(3):
            acc = acc + got[b // 2, d].astype(F32)
        t1[b // 2] = acc.astype(BF)
        for d in (1, 2, 3):
            xd, zd = step(x, d), step(z, d)
            if b % 2 == 0:
                src, to = t1.at[b // 2, zd // 2, lax.rem(zd, 2)], along_z[d - 1]
            else:
                src, to = t1.at[b // 2, xd], along_x[d - 1]
            copies.append(rdma(src, r2.at[b, d - 1], 16 + 3 * b + d - 1, to))
        return copies

    def assemble(which, dst):
        for copy in halo_out[which]:
            copy.wait()
        pack[...] = recv_out[which].astype(F32)
        for l in range(2):
            for a in range(24):
                i, ar = (a - 3) // 6, (a - 3) % 6
                at_ = l * 24 + a
                if a < 3:
                    n = l * 3 + a
                    rows_s[at_, 6:18] = pack[S_AT + n * 12 : S_AT + n * 12 + 12]
                    rows_s[at_, 18:24] = pack[S_AT + 72 + n * 6 : S_AT + 72 + n * 6 + 6]
                    rows_s[at_, 0:6] = pack[C_AT + n * 6 : C_AT + n * 6 + 6]
                else:
                    n = l * 6 + ar if i < 3 else l * 3 + ar
                    rows_s[at_, 0:6] = pack[E_AT + 72 * i + n * 6 : E_AT + 72 * i + n * 6 + 6]
                    rows_s[at_, 6:18] = wide[which, window_of(i, 0), n * 12 : n * 12 + 12]
                    rows_s[at_, 18:24] = wide[which, window_of(i, 1), n * 6 : n * 6 + 6]
                dst[l, a] = rows_s[at_].astype(BF)

    stage2 = [second_axis(0), second_axis(1)]
    assemble(0, of_ref)
    stage2 += [second_axis(2), second_axis(3)]
    assemble(1, df_ref)

    for b in range(4):
        for copy in stage2[b]:
            copy.wait()
        if b % 2 == 0:
            acc = t1x[b // 2, zh, zl].astype(F32)
        else:
            acc = t1z[b // 2, x].astype(F32)
        for d in range(3):
            acc = acc + r2[b, d].astype(F32)
        tc[...] = acc
        for k in range(4):
            t3f[k, 4 * b : 4 * b + 4] = tc[4 * k : 4 * k + 4]
    t3[...] = t3f[...].astype(BF)
    stage3 = [rdma(t3.at[step(y, d)], r3.at[d - 1], 28 + d - 1, along_y[d - 1]) for d in (1, 2, 3)]
    for copy in stage3:
        copy.wait()
    acc = t3f[y]
    for d in range(3):
        acc = acc + r3[d].astype(F32)
    tc[...] = acc
    for b in range(3):
        qg_ref[:, 512 * b : 512 * b + 512] = tc[4 * b : 4 * b + 4]
    og_ref[...] = tc[12:16]


def shards(fields, cotangent, qkv_weight, out_weight):
    vm = pl.BlockSpec(memory_space=pltpu.VMEM)
    return tuple(
        pl.pallas_call(
            kernel,
            out_shape=[
                jax.ShapeDtypeStruct((2, 24, 24, D), BF),
                jax.ShapeDtypeStruct((2, 24, 24, D), BF),
                jax.ShapeDtypeStruct((4, 3 * D), F32),
                jax.ShapeDtypeStruct((4, D), F32),
            ],
            in_specs=[vm] * 4,
            out_specs=[vm] * 4,
            scratch_shapes=[
                pltpu.VMEM((2, NW, T, D), F32),
                pltpu.VMEM((48, 24, D), F32),
                pltpu.VMEM((MSG, D), F32),
            ]
            + [pltpu.VMEM((2, MSG, D), BF)] * 4
            + [pltpu.SemaphoreType.DMA((2, 3))] * 4
            + [pltpu.VMEM((TOK, D), BF)] * 3
            + [pltpu.VMEM((2, TOK, 256), BF)] * 4
            + [
                pltpu.VMEM((TOK, D), BF),
                pltpu.VMEM((TOK, 3 * D), BF),
                pltpu.VMEM((3 * D, D), BF),
                pltpu.VMEM((D, D), BF),
                pltpu.VMEM((4, 2, 4, 2, 2, 16, 512), BF),
                pltpu.VMEM((4, 2, 4, 2, 16, 512), BF),
                pltpu.VMEM((4, 2, 4, 2, 16, 512), BF),
                pltpu.VMEM((2, 3, 2, 2, 16, 512), BF),
                pltpu.VMEM((2, 3, 4, 16, 512), BF),
                pltpu.VMEM((2, 2, 2, 16, 512), BF),
                pltpu.VMEM((2, 4, 16, 512), BF),
                pltpu.VMEM((4, 3, 16, 512), BF),
                pltpu.VMEM((16, D), F32),
                pltpu.VMEM((4, 16, D), F32),
                pltpu.VMEM((4, 16, D), BF),
                pltpu.VMEM((3, 16, D), BF),
                pltpu.SemaphoreType.DMA((31,)),
                pltpu.SemaphoreType.DMA((31,)),
            ],
            compiler_params=pltpu.CompilerParams(
                collective_id=0, has_side_effects=True, vmem_limit_bytes=58 * 1024 * 1024
            ),
            cost_estimate=pl.CostEstimate(flops=10 * 10**9, bytes_accessed=8 * 10**6, transcendentals=3 * 10**6),
        )(fields, cotangent, qkv_weight, out_weight)
    )


def solution(mesh):
    placed = (P(None, "lat", "lon", None), P(None, "lat", "lon", None), P(), P())
    return jax.shard_map(
        shards,
        mesh=mesh,
        in_specs=placed,
        out_specs=(
            P(None, "lat", "lon", None),
            P(None, "lat", "lon", None),
            P(("lon", "lat"), None),
            P(("lon", "lat"), None),
        ),
        check_vma=False,
    )
```

time: 410 us -> 69.3 us (0.17); the launches traced: 403 us -> 69.2 us
  waiting for transfers between devices: 142 us -> 0 us
  matrix products: 89 us -> 0 us
  local copies, waits for them, and re-layouts: 85.8 us -> 4.69 us
  Pallas kernels: 0 us -> 63.9 us
  other arithmetic: 59.1 us -> 0 us
  between operations: 14.7 us -> 0.65 us
  starting transfers between devices: 11.9 us -> 0 us
    unnamed x2 -> x0, waiting for transfers between devices: 123 us -> none
    dot_general x12 -> x0, matrix products: 89 us -> none  [the longest x3 39.4 us: attend(): jnp.einsum('wqhe,wkhe->whqk', queries, keyset, preferred_element_type=jnp...]
    pallas_call x0 -> x1, Pallas kernels: none -> 63.9 us  [shards(): pl.pallas_call(kernel, out_shape=[jax.ShapeDtypeStruct((2, 24, 24, D), BF...]
    reduce_sum x5 -> x0, other arithmetic: 42.5 us -> none  [the longest x1 20.4 us: attend(): raised = jnp.exp(scores - highest)]
    convert_element_type x8 -> x0, local copies, waits for them, and re-layouts: 23.8 us -> none  [the longest x3 11 us: shards(): tokens_flat.astype(jnp.float32)]
    slice x12 -> x0, local copies, waits for them, and re-layouts: 20.2 us -> none  [the longest x8 8.63 us: roll_grid(): leading, trailing = (field[:, :cutoff], field[:, cutoff:])]
    ppermute x8 -> x0, waiting for transfers between devices: 19.3 us -> none  [from_behind(): lax.ppermute(x, axis, [(i, (i + by) % length) for i in range(length)])]
    reshape x4 -> x0, local copies, waits for them, and re-layouts: 15 us -> none  [the longest x1 3.85 us: attend(): projected[..., :width].reshape(wincount, tokens_win, HEADS, head_size)]
  transfers between devices with their start and end apart: 9 -> 0, of which waited for: 5 -> 0; matrix products, arithmetic and copies ran while one was open for 14% -> 0% of each run, Pallas kernels for 0% -> 0%
where the time goes in v1:
time: 69.3 us; the launch traced here: 69.2 us
  Pallas kernels  63.9 us (92%)
  local copies, waits for them, and re-layouts  4.69 us (7%)
    pallas_call x1, Pallas kernels, shards(): pl.pallas_call(kernel, out_shape=[jax.ShapeDtypeStruct((2, 24, 24, D), BF...  63.9 us
    unnamed x10, local copies, waits for them, and re-layouts  4.69 us

profile of v1, /device:TPU:0, one launch (start us, length us, event | category | flops | bytes accessed | tf_op | source)
XLA Modules:
  0.0 69.2 jit_solution(7458601741124636294)
XLA Ops:
  0.6 63.9 %shard_map.75 = (bf16[2,24,24,512]{3,2,1,0:T(8,128)(2,1)}, bf16[2,24,24,512]{3,2,1,0:T(8,128)(2,1)}, f32[4,1536]{1,0:T(4,128)}, f32[4,512]{1,0:T(4,128)}) custom-call(bf16[2,24,24,512]{3,2,1,0:T(8,128)(2,1)} %f_ref.1, bf16[2,24,24,512]{3,2,1,0:T(8,128)(2,1)} %c_ref.1, bf16[512,1536]{1,0:T(8,128)(2,1)} %w_ref.1, bf16[512,512]{1,0:T(8,128)(2,1)} %wo_ref.1), custom_call_target="tpu_custom_call" | custom-call | flops 10000000000 | bytes 8000000 | tf_op jit(solution)/shard_map/pallas_call | solution.py:383
  64.5 0.0 copy-start
  64.5 2.5 %copy.12 = bf16[2,24,24,512]{3,2,1,0:T(8,128)(2,1)} copy(bf16[2,24,24,512]{3,2,1,0:T(8,128)(2,1)} %get-tuple-element.8) | data formatting | bytes 2359296
  67.0 0.0 copy-done
  67.0 0.0 copy-start.1
  67.0 0.0 copy-start.2
  67.0 1.0 %copy.13 = bf16[2,24,24,512]{3,2,1,0:T(8,128)(2,1)} copy(bf16[2,24,24,512]{3,2,1,0:T(8,128)(2,1)S(1)} %copy-done) | data formatting | bytes 2359296
  68.0 0.0 copy-done.1
  68.0 0.6 copy.14
  68.6 0.0 copy-done.2
  68.6 0.6 copy.15
Async XLA Ops:
  64.5 2.5 %copy-start = (bf16[2,24,24,512]{3,2,1,0:T(8,128)(2,1)S(1)}, bf16[2,24,24,512]{3,2,1,0:T(8,128)(2,1)}, u32[]{:S(2)}) copy-start(bf16[2,24,24,512]{3,2,1,0:T(8,128)(2,1)} %get-tuple-element.9) | copy-start | bytes 3538948
  67.0 1.0 %copy-start.1 = (f32[4,1536]{1,0:T(4,128)S(1)}, f32[4,1536]{1,0:T(4,128)}, u32[]{:S(2)}) copy-start(f32[4,1536]{1,0:T(4,128)} %get-tuple-element.10) | copy-start | bytes 73732
  67.0 1.6 %copy-start.2 = (f32[4,512]{1,0:T(4,128)S(1)}, f32[4,512]{1,0:T(4,128)}, u32[]{:S(2)}) copy-start(f32[4,512]{1,0:T(4,128)} %get-tuple-element.11) | copy-start | bytes 24580

commit v2 on v1

v2 whole, which is shorter than its diff:
```python
import functools, math
import jax
import jax.numpy as jnp
from jax import lax
from jax.experimental import pallas as pl
from jax.experimental.pallas import tpu as pltpu
from jax.sharding import PartitionSpec as P

D = 512
HEADS = 16
HD = 32
T = 144
NW = 8
TOK = NW * T
F32 = jnp.float32
BF = jnp.bfloat16
EPS = 1e-5
SCALE = HD ** -0.5
LOG2E = math.log2(math.e)
LN2 = math.log(2.0)


def nt(a, b):
    return lax.dot_general(a, b, (((1,), (1,)), ((), ())), preferred_element_type=F32)


def nn(a, b):
    return lax.dot_general(a, b, (((1,), (0,)), ((), ())), preferred_element_type=F32)


def tn(a, b):
    return lax.dot_general(a, b, (((0,), (0,)), ((), ())), preferred_element_type=F32)


def norm_stats(x):
    mean = jnp.sum(x, axis=-1, keepdims=True) * (1.0 / D)
    xc = x - mean
    var = jnp.sum(xc * xc, axis=-1, keepdims=True) * (1.0 / D)
    return xc, lax.rsqrt(var + EPS)


def heads_apart(a):
    lane = lax.broadcasted_iota(jnp.int32, (1, 128), 1) // HD
    zero = jnp.zeros((T, 128), BF)
    parts = []
    for h in range(8):
        mask = jnp.where(lane == h % 4, 1.0, 0.0).astype(BF)
        own = a[:, 128 * (h // 4) : 128 * (h // 4) + 128] * mask
        parts.append(jnp.concatenate([own, zero] if h < 4 else [zero, own], axis=1))
    return jnp.concatenate(parts, axis=0)


def heads_together(a):
    lane = lax.broadcasted_iota(jnp.int32, (1, 128), 1) // HD
    halves = []
    for c in range(2):
        cols = slice(128 * c, 128 * c + 128)
        own = a[T * 4 * c : T * 4 * c + T, cols]
        for h in range(1, 4):
            at = T * (4 * c + h)
            own = jnp.where(lane == h, a[at : at + T, cols], own)
        halves.append(own)
    return jnp.concatenate(halves, axis=1)


def attention(w, big, q_s, k_s, v_s, p_s, o_s):
    rows = pl.ds(pl.multiple_of(w * T, 16), T)
    half = T // 2
    query = lax.broadcasted_iota(jnp.int32, (1, 8 * T), 1) % T
    pen0 = jnp.where(query >= half, big, 0.0)
    pen1 = jnp.where(query < half, big, 0.0)
    for g in range(2):
        st = nt(k_s[g, rows, :], heads_apart(q_s[g, rows, :]))
        top = jnp.maximum(
            jnp.max(st[:half], axis=0, keepdims=True) - pen0, jnp.max(st[half:], axis=0, keepdims=True) - pen1
        )
        e = jnp.concatenate([jnp.exp2(st[:half] - (top + pen0)), jnp.exp2(st[half:] - (top + pen1))], axis=0)
        pb = (e * (1.0 / jnp.sum(e, axis=0, keepdims=True))).astype(BF)
        p_s[w, g] = pb
        o_s[rows, 256 * g : 256 * g + 256] = heads_together(tn(pb, v_s[g, rows, :])).astype(BF)


def attention_back(w, q_s, k_s, v_s, p_s, do_s, dp_s):
    rows = pl.ds(pl.multiple_of(w * T, 16), T)
    for g in range(2):
        kg = k_s[g, rows, :]
        qm = heads_apart(q_s[g, rows, :])
        dom = heads_apart(do_s[g, rows, :])
        dpt = nt(v_s[g, rows, :], dom)
        pb = p_s[w, g]
        p = pb.astype(F32)
        ds = (p * (dpt - jnp.sum(p * dpt, axis=0, keepdims=True))).astype(BF)
        dp_s[rows, 1024 + 256 * g : 1280 + 256 * g] = nn(pb, dom).astype(BF)
        dp_s[rows, 512 + 256 * g : 768 + 256 * g] = (nn(ds, qm) * LN2).astype(BF)
        dp_s[rows, 256 * g : 256 * g + 256] = (heads_together(tn(ds, kg)) * SCALE).astype(BF)


MESH = pl.DeviceIdType.MESH
E_AT, S_AT, C_AT, MSG = 0, 256, 368, 416
PARTS = ((E_AT, 256), (S_AT, 112), (C_AT, 48))
FREE = 3 * T


def window_of(i, j):
    if i < 3:
        return i + 3 * j
    return 6 + j


def neighbours(by):
    lon, lat = lax.axis_index("lon"), lax.axis_index("lat")
    nlon, nlat = lax.axis_size("lon"), lax.axis_size("lat")
    lon2, lat2 = lax.rem(lon + by + nlon, nlon), lax.rem(lat + by + nlat, nlat)
    return [(lon2, lat), (lon, lat2), (lon2, lat2)]


def halo_copies(which, send, recv, send_sem, recv_sem, to):
    return [
        pltpu.make_async_remote_copy(
            src_ref=send.at[which, pl.ds(at, rows)],
            dst_ref=recv.at[which, pl.ds(at, rows)],
            send_sem=send_sem.at[which, n],
            recv_sem=recv_sem.at[which, n],
            device_id=peer,
            device_id_type=MESH,
        )
        for n, ((at, rows), peer) in enumerate(zip(PARTS, to))
    ]


def kernel(
    f_any, c_any, w_any, wo_any, of_ref, df_ref, qg_ref, og_ref,
    f_ref, c_ref, w_ref, wo_ref, load_sem,
    wide, rows_s, pack, send_in, recv_in, send_out, recv_out, in_send, in_recv, out_send, out_recv,
    xw, gw, xn_s, q_s, k_s, v_s, do_s, o_s, dp_s, p_s, wt_s, wot_s,
    wg, r0, cut, t0, r1, t1, r2, t2, r3, t3, rs_send, rs_recv,
):
    lon, lat = lax.axis_index("lon"), lax.axis_index("lat")
    core, x, zh = lax.rem(lon, 2), lax.rem(lon // 2, 4), lon // 8
    y, zl = lax.rem(lat, 4), lat // 4
    z = zh * 2 + zl

    def at(zh_, x_, core_, zl_, y_):
        return ((zh_ * 4 + x_) * 2 + core_, zl_ * 4 + y_)

    def step(v, d):
        return lax.rem(v + d, 4)

    partner = at(zh, x, 1 - core, zl, y)
    position = {"x": x, "y": y, "z": z}
    along = {
        "x": [at(zh, step(x, d), core, zl, y) for d in (1, 2, 3)],
        "y": [at(zh, x, core, zl, step(y, d)) for d in (1, 2, 3)],
        "z": [at(step(z, d) // 2, x, core, lax.rem(step(z, d), 2), y) for d in (1, 2, 3)],
    }
    ahead, behind = neighbours(1), neighbours(-1)
    peers = ahead + behind + [partner] + along["x"] + along["y"] + along["z"]
    barrier = pltpu.get_barrier_semaphore()
    for peer in peers:
        pl.semaphore_signal(barrier, inc=1, device_id=peer, device_id_type=MESH)
    loads = [
        pltpu.make_async_copy(src, dst, load_sem.at[n])
        for n, (src, dst) in enumerate(((f_any, f_ref), (c_any, c_ref), (w_any, w_ref), (wo_any, wo_ref)))
    ]
    for load in loads:
        load.start()

    halo_in = []

    def pack_in(which, src):
        loads[which].wait()
        for l in range(2):
            for a in range(24):
                i, ar = (a - 3) // 6, (a - 3) % 6
                if a < 3:
                    row = src[l, a].astype(F32)
                    n = l * 3 + a
                    pack[S_AT + n * 12 : S_AT + n * 12 + 12] = row[6:18]
                    pack[S_AT + 72 + n * 6 : S_AT + 72 + n * 6 + 6] = row[18:24]
                    pack[C_AT + n * 6 : C_AT + n * 6 + 6] = row[0:6]
                else:
                    row = src[l, a, 0:16].astype(F32)
                    n = l * 6 + ar if i < 3 else l * 3 + ar
                    pack[E_AT + 72 * i + n * 6 : E_AT + 72 * i + n * 6 + 6] = row[0:6]
        send_in[which] = pack[...].astype(BF)

    def send(which):
        halo_in.append(halo_copies(which, send_in, recv_in, in_send, in_recv, behind))
        for copy in halo_in[-1]:
            copy.start()

    def own(which, src):
        for l in range(2):
            for a in range(3, 24):
                i, ar = (a - 3) // 6, (a - 3) % 6
                row = src[l, a].astype(F32)
                n = l * 6 + ar if i < 3 else l * 3 + ar
                wide[which, window_of(i, 0), n * 12 : n * 12 + 12] = row[6:18]
                wide[which, window_of(i, 1), n * 6 : n * 6 + 6] = row[18:24]

    pack_in(0, f_ref)
    own(0, f_ref)
    pl.semaphore_wait(barrier, len(peers))
    send(0)
    pack_in(1, c_ref)
    own(1, c_ref)
    loads[2].wait()
    loads[3].wait()
    wt_s[...] = w_ref[...].T
    wot_s[...] = wo_ref[...].T

    def project(first, count):
        rows = slice(first * T, (first + count) * T)
        for w in range(first, first + count):
            at_ = slice(w * T, w * T + T)
            xv = wide[0, w]
            xw[at_] = xv.astype(BF)
            xc, rstd = norm_stats(xv)
            xn_s[at_] = (xc * rstd).astype(BF)
        for part, (dst, scale) in enumerate(((q_s, SCALE * LOG2E), (k_s, None), (v_s, None))):
            for n in range(2):
                res = nn(xn_s[rows], w_ref[:, 512 * part + 256 * n : 512 * part + 256 * n + 256])
                if scale is not None:
                    res = res * scale
                dst[n, rows] = res.astype(BF)

    last = jnp.where(lat == lax.axis_size("lat") - 1, 1e9, 0.0)

    def attend(first, count):
        def window(w, _):
            big = jnp.where(w >= NW - 2, last, 0.0).astype(F32)
            attention(w, big, q_s, k_s, v_s, p_s, o_s)
            return 0

        lax.fori_loop(first, first + count, window, 0)

    def attend_back(first, count):
        def window(w, _):
            attention_back(w, q_s, k_s, v_s, p_s, do_s, dp_s)
            return 0

        lax.fori_loop(first, first + count, window, 0)

    def finish_out(first, count):
        for w in range(first, first + count):
            at_ = slice(w * T, w * T + T)
            wide[0, w] = xw[at_].astype(F32) + nn(o_s[at_], wo_ref[...])

    def finish_grad(first, count):
        for w in range(first, first + count):
            at_ = slice(w * T, w * T + T)
            gn = nn(dp_s[at_], wt_s[...])
            xc, rstd = norm_stats(xw[at_].astype(F32))
            xh = xc * rstd
            m1 = jnp.sum(gn, axis=-1, keepdims=True) * (1.0 / D)
            m2 = jnp.sum(gn * xh, axis=-1, keepdims=True) * (1.0 / D)
            wide[1, w] = gw[at_].astype(F32) + rstd * (gn - m1 - xh * m2)

    def halo_arrived(which):
        for copy in halo_in[which]:
            copy.wait()
        pack[...] = recv_in[which].astype(F32)
        for i in range(3):
            wide[which, 3 + i, 72:144] = pack[E_AT + 72 * i : E_AT + 72 * i + 72]
        wide[which, 7, 36:72] = pack[E_AT + 216 : E_AT + 252]
        wide[which, 6, 72:144] = pack[S_AT : S_AT + 72]
        wide[which, 7, 72:108] = pack[S_AT + 72 : S_AT + 108]
        wide[which, 7, 108:144] = pack[C_AT : C_AT + 36]

    halo_out = []

    def send_back(which):
        for i in range(3):
            pack[E_AT + 72 * i : E_AT + 72 * i + 72] = wide[which, 3 + i, 72:144]
        pack[E_AT + 216 : E_AT + 252] = wide[which, 7, 36:72]
        pack[S_AT : S_AT + 72] = wide[which, 6, 72:144]
        pack[S_AT + 72 : S_AT + 108] = wide[which, 7, 72:108]
        pack[C_AT : C_AT + 36] = wide[which, 7, 108:144]
        send_out[which] = pack[...].astype(BF)
        halo_out.append(halo_copies(which, send_out, recv_out, out_send, out_recv, ahead))
        for copy in halo_out[-1]:
            copy.start()

    orders = ("xzy", "zyx", "yxz", "xzy")
    going = [None] * 4

    def rdma(b, n, src, dst, peer):
        copy = pltpu.make_async_remote_copy(
            src_ref=src, dst_ref=dst, send_sem=rs_send.at[b, n], recv_sem=rs_recv.at[b, n],
            device_id=peer, device_id_type=MESH,
        )
        copy.start()
        return copy

    def term(b):
        res = tn(xn_s[...], dp_s[:, 512 * b : 512 * b + 512]) if b < 3 else tn(o_s[...], gw[...])
        wg[b] = res.astype(BF).reshape(2, 4, 2, 2, 16, 512)
        going[b] = [rdma(b, 0, wg.at[b, :, :, 1 - core], r0.at[b], partner)]

    def pick(dims, axis, i):
        return tuple(i if dim == axis else slice(None) for dim in dims)

    def stage(b, n):
        for copy in going[b]:
            copy.wait()
        order, dims = orders[b], "zxy"
        held, got = (t0, t1, t2), (r1, r2, r3)
        if n == 0:
            for i in range(2):
                for k in range(4):
                    cut[i, k] = wg[b, i, k, core].astype(F32) + r0[b, i, k].astype(F32)
            for i in range(2):
                for j in range(2):
                    for k in range(4):
                        for m in range(4):
                            t3[2 * i + j, :, k, 4 * m : 4 * m + 4] = cut[i, :, j, 4 * k : 4 * k + 4, 128 * m : 128 * m + 128]
            t0[b] = t3[...].astype(BF)
        else:
            for axis in order[: n - 1]:
                dims = dims.replace(axis, "")
            axis = order[n - 1]
            acc = held[n - 1][(b, *pick(dims, axis, position[axis]))].astype(F32)
            for d in range(3):
                acc = acc + got[n - 1][b, d].astype(F32)
            if n == 3:
                out, first = (qg_ref, 512 * b) if b < 3 else (og_ref, 0)
                for m in range(4):
                    out[:, first + 128 * m : first + 128 * m + 128] = acc[4 * m : 4 * m + 4]
                return
            held[n][b] = acc.astype(BF)
            dims = dims.replace(axis, "")
        axis = order[n]
        going[b] = [
            rdma(b, 3 * n + d, held[n].at[(b, *pick(dims, axis, step(position[axis], d)))], got[n].at[b, d - 1], along[axis][d - 1])
            for d in (1, 2, 3)
        ]

    project(0, 3)
    send(1)
    attend(0, 3)
    halo_arrived(0)
    project(3, 5)
    attend(3, 5)
    finish_out(3, 5)
    send_back(0)
    halo_arrived(1)
    for w in range(NW):
        gw[w * T : w * T + T] = wide[1, w].astype(BF)
    term(3)
    finish_out(0, 3)
    for n in range(2):
        do_s[n] = nn(gw[...], wot_s[:, 256 * n : 256 * n + 256]).astype(BF)
    attend_back(3, 1)
    stage(3, 0)
    attend_back(4, 4)
    finish_grad(3, 5)
    send_back(1)
    stage(3, 1)
    attend_back(0, 3)
    term(0)
    term(1)
    stage(0, 0)
    term(2)
    stage(1, 0)
    stage(3, 2)
    finish_grad(0, 3)
    stage(2, 0)

    def assemble(which, dst):
        for copy in halo_out[which]:
            copy.wait()
        pack[...] = recv_out[which].astype(F32)
        for l in range(2):
            for a in range(24):
                i, ar = (a - 3) // 6, (a - 3) % 6
                at_ = l * 24 + a
                if a < 3:
                    n = l * 3 + a
                    rows_s[at_, 6:18] = pack[S_AT + n * 12 : S_AT + n * 12 + 12]
                    rows_s[at_, 18:24] = pack[S_AT + 72 + n * 6 : S_AT + 72 + n * 6 + 6]
                    rows_s[at_, 0:6] = pack[C_AT + n * 6 : C_AT + n * 6 + 6]
                else:
                    n = l * 6 + ar if i < 3 else l * 3 + ar
                    rows_s[at_, 0:6] = pack[E_AT + 72 * i + n * 6 : E_AT + 72 * i + n * 6 + 6]
                    rows_s[at_, 6:18] = wide[which, window_of(i, 0), n * 12 : n * 12 + 12]
                    rows_s[at_, 18:24] = wide[which, window_of(i, 1), n * 6 : n * 6 + 6]
                dst[l, a] = rows_s[at_].astype(BF)

    assemble(0, of_ref)
    for n in (1, 2):
        for b in range(3):
            stage(b, n)
        if n == 1:
            assemble(1, df_ref)
    for b in range(4):
        stage(b, 3)


def shards(fields, cotangent, qkv_weight, out_weight):
    vm = pl.BlockSpec(memory_space=pltpu.VMEM)
    results = list(
        pl.pallas_call(
            kernel,
            out_shape=[
                pltpu.VMEM((2, 24, 24, D), BF),
                pltpu.VMEM((2, 24, 24, D), BF),
                pltpu.VMEM((4, 3 * D), F32),
                pltpu.VMEM((4, D), F32),
            ],
            in_specs=[pl.BlockSpec(memory_space=pl.ANY)] * 4,
            out_specs=[vm] * 4,
            scratch_shapes=[
                pltpu.VMEM((2, 24, 24, D), BF),
                pltpu.VMEM((2, 24, 24, D), BF),
                pltpu.VMEM((D, 3 * D), BF),
                pltpu.VMEM((D, D), BF),
                pltpu.SemaphoreType.DMA((4,)),
                pltpu.VMEM((2, NW, T, D), F32),
                pltpu.VMEM((48, 24, D), F32),
                pltpu.VMEM((MSG, D), F32),
            ]
            + [pltpu.VMEM((2, MSG, D), BF)] * 4
            + [pltpu.SemaphoreType.DMA((2, 3))] * 4
            + [pltpu.VMEM((TOK, D), BF)] * 3
            + [pltpu.VMEM((2, TOK, 256), BF)] * 4
            + [
                pltpu.VMEM((TOK, D), BF),
                pltpu.VMEM((TOK, 3 * D), BF),
                pltpu.VMEM((NW, 2, T, 8 * T), BF),
                pltpu.VMEM((3 * D, D), BF),
                pltpu.VMEM((D, D), BF),
                pltpu.VMEM((4, 2, 4, 2, 2, 16, 512), BF),
                pltpu.VMEM((4, 2, 4, 2, 16, 512), BF),
                pltpu.VMEM((2, 4, 2, 16, 512), F32),
                pltpu.VMEM((4, 4, 4, 4, 16, 128), BF),
                pltpu.VMEM((4, 3, 4, 4, 16, 128), BF),
                pltpu.VMEM((4, 4, 4, 16, 128), BF),
                pltpu.VMEM((4, 3, 4, 16, 128), BF),
                pltpu.VMEM((4, 4, 16, 128), BF),
                pltpu.VMEM((4, 3, 16, 128), BF),
                pltpu.VMEM((4, 4, 4, 16, 128), F32),
                pltpu.SemaphoreType.DMA((4, 10)),
                pltpu.SemaphoreType.DMA((4, 10)),
            ],
            compiler_params=pltpu.CompilerParams(
                collective_id=0, has_side_effects=True, vmem_limit_bytes=58 * 1024 * 1024
            ),
            cost_estimate=pl.CostEstimate(flops=10 * 10**9, bytes_accessed=8 * 10**6, transcendentals=3 * 10**6),
        )(fields, cotangent, qkv_weight, out_weight)
    )

    def hand_over(*refs):
        copies = [pltpu.make_async_copy(refs[n], refs[4 + n], refs[8].at[n]) for n in range(4)]
        for copy in copies:
            copy.start()
        for copy in copies:
            copy.wait()

    return tuple(
        pl.pallas_call(
            hand_over,
            out_shape=[jax.ShapeDtypeStruct(r.shape, r.dtype) for r in results],
            in_specs=[vm] * 4,
            out_specs=[pl.BlockSpec(memory_space=pl.ANY)] * 4,
            scratch_shapes=[pltpu.SemaphoreType.DMA((4,))],
        )(*[pltpu.with_memory_space_constraint(r, pltpu.VMEM) for r in results])
    )


def solution(mesh):
    placed = (P(None, "lat", "lon", None), P(None, "lat", "lon", None), P(), P())
    return jax.shard_map(
        shards,
        mesh=mesh,
        in_specs=placed,
        out_specs=(
            P(None, "lat", "lon", None),
            P(None, "lat", "lon", None),
            P(("lon", "lat"), None),
            P(("lon", "lat"), None),
        ),
        check_vma=False,
    )
```

time: 69.3 us -> 60.1 us (0.87)
  Pallas kernels: 63.9 us -> 59.1 us
  local copies, waits for them, and re-layouts: 4.69 us -> 0 us
    pallas_call x1 -> x2, Pallas kernels: 63.9 us -> 59.1 us  [the longest x1 57.7 us: shards(): pl.pallas_call(kernel, out_shape=[pltpu.VMEM((2, 24, 24, D), BF), pltpu.V...]
    unnamed x10 -> x0, local copies, waits for them, and re-layouts: 4.69 us -> none
where the time goes in v2:
time: 60.1 us; the launch traced here: 59.9 us
  Pallas kernels  59.1 us (98%)
  between operations  0.8 us (1%)
    pallas_call x1, Pallas kernels, shards(): pl.pallas_call(kernel, out_shape=[pltpu.VMEM((2, 24, 24, D), BF), pltpu.V...  57.7 us
    pallas_call x1, Pallas kernels, shards(): pl.pallas_call(hand_over, out_shape=[jax.ShapeDtypeStruct(r.shape, r.dtyp...  1.44 us

profile of v2, /device:TPU:0, one launch (start us, length us, event | category | flops | bytes accessed | tf_op | source)
XLA Modules:
  0.0 59.9 jit_solution(12010059020864501632)
XLA Ops:
  0.6 57.7 %shard_map.75 = (bf16[2,24,24,512]{3,2,1,0:T(8,128)(2,1)S(1)}, bf16[2,24,24,512]{3,2,1,0:T(8,128)(2,1)S(1)}, f32[4,1536]{1,0:T(4,128)S(1)}, f32[4,512]{1,0:T(4,128)S(1)}) custom-call(bf16[2,24,24,512]{3,2,1,0:T(8,128)(2,1)} %f_any.1, bf16[2,24,24,512]{3,2,1,0:T(8,128)(2,1)} %c_any.1, bf16[512,1536]{1,0:T(8,128)(2,1)} %w_any.1, bf16[512,512]{1,0:T(8,128)(2,1)} %wo_any.1), custom_call_target="tpu_custom_call" | custom-call | flops 10000000000 | bytes 8000000 | tf_op jit(solution)/shard_map/pallas_call | solution.py:402
  58.3 1.4 %shard_map.76 = (bf16[2,24,24,512]{3,2,1,0:T(8,128)(2,1)}, bf16[2,24,24,512]{3,2,1,0:T(8,128)(2,1)}, f32[4,1536]{1,0:T(4,128)}, f32[4,512]{1,0:T(4,128)}) custom-call(bf16[2,24,24,512]{3,2,1,0:T(8,128)(2,1)S(1)} %get-tuple-element.8.refs_0_, bf16[2,24,24,512]{3,2,1,0:T(8,128)(2,1)S(1)} %get-tuple-element.9.refs_1_, f32[4,1536]{1,0:T(4,128)S(1)} %get-tuple-element.10.refs_2_, ...), custom_call_target="tpu_custom_call" | custom-call | tf_op jit(solution)/shard_map/pallas_call | solution.py:460

commit v3 on v2

--- a/solution.py
+++ b/solution.py
@@ -133,7 +133,7 @@
     f_ref, c_ref, w_ref, wo_ref, load_sem,
     wide, rows_s, pack, send_in, recv_in, send_out, recv_out, in_send, in_recv, out_send, out_recv,
     xw, gw, xn_s, q_s, k_s, v_s, do_s, o_s, dp_s, p_s, wt_s, wot_s,
-    wg, r0, cut, t0, r1, t1, r2, t2, r3, t3, rs_send, rs_recv,
+    wg, r0, cut, t0, r1, t1, r2, t3, rs_send, rs_recv,
 ):
     lon, lat = lax.axis_index("lon"), lax.axis_index("lat")
     core, x, zh = lax.rem(lon, 2), lax.rem(lon // 2, 4), lon // 8
@@ -155,6 +155,12 @@
     }
     ahead, behind = neighbours(1), neighbours(-1)
     peers = ahead + behind + [partner] + along["x"] + along["y"] + along["z"]
+    for m in (1, 2, 3):
+        for n in (1, 2, 3):
+            zn = step(z, n)
+            peers.append(at(zh, step(x, m), core, zl, step(y, n)))
+            peers.append(at(zn // 2, step(x, m), core, lax.rem(zn, 2), y))
+            peers.append(at(zn // 2, x, core, lax.rem(zn, 2), step(y, m)))
     barrier = pltpu.get_barrier_semaphore()
     for peer in peers:
         pl.semaphore_signal(barrier, inc=1, device_id=peer, device_id_type=MESH)
@@ -234,6 +240,13 @@
 
         lax.fori_loop(first, first + count, window, 0)
 
+    def project_grad(first, count):
+        rows = slice(first * T, (first + count) * T)
+        for w in range(first, first + count):
+            gw[w * T : w * T + T] = wide[1, w].astype(BF)
+        for n in range(2):
+            do_s[n, rows] = nn(gw[rows], wot_s[:, 256 * n : 256 * n + 256]).astype(BF)
+
     def attend_back(first, count):
         def window(w, _):
             attention_back(w, q_s, k_s, v_s, p_s, do_s, dp_s)
@@ -281,7 +294,7 @@
         for copy in halo_out[-1]:
             copy.start()
 
-    orders = ("xzy", "zyx", "yxz", "xzy")
+    axes = ("x", "z", "y", "x")
     going = [None] * 4
 
     def rdma(b, n, src, dst, peer):
@@ -300,11 +313,14 @@
     def pick(dims, axis, i):
         return tuple(i if dim == axis else slice(None) for dim in dims)
 
+    def device(spot):
+        return at(spot["z"] // 2, spot["x"], core, lax.rem(spot["z"], 2), spot["y"])
+
     def stage(b, n):
         for copy in going[b]:
             copy.wait()
-        order, dims = orders[b], "zxy"
-        held, got = (t0, t1, t2), (r1, r2, r3)
+        axis = axes[b]
+        p, q = "zxy".replace(axis, "")
         if n == 0:
             for i in range(2):
                 for k in range(4):
@@ -315,56 +331,57 @@
                         for m in range(4):
                             t3[2 * i + j, :, k, 4 * m : 4 * m + 4] = cut[i, :, j, 4 * k : 4 * k + 4, 128 * m : 128 * m + 128]
             t0[b] = t3[...].astype(BF)
+            going[b] = [
+                rdma(b, d, t0.at[(b, *pick("zxy", axis, step(position[axis], d)))], r1.at[b, d - 1], along[axis][d - 1])
+                for d in (1, 2, 3)
+            ]
+        elif n == 1:
+            acc = t0[(b, *pick("zxy", axis, position[axis]))].astype(F32)
+            for d in range(3):
+                acc = acc + r1[b, d].astype(F32)
+            t1[b] = acc.astype(BF)
+            going[b] = []
+            for m in range(15, 0, -1):
+                spot = dict(position)
+                spot[p], spot[q] = step(position[p], m // 4), step(position[q], m % 4)
+                going[b].append(rdma(b, 3 + m, t1.at[b, spot[p], spot[q]], r2.at[b, m - 1], device(spot)))
         else:
-            for axis in order[: n - 1]:
-                dims = dims.replace(axis, "")
-            axis = order[n - 1]
-            acc = held[n - 1][(b, *pick(dims, axis, position[axis]))].astype(F32)
-            for d in range(3):
-                acc = acc + got[n - 1][b, d].astype(F32)
-            if n == 3:
-                out, first = (qg_ref, 512 * b) if b < 3 else (og_ref, 0)
-                for m in range(4):
-                    out[:, first + 128 * m : first + 128 * m + 128] = acc[4 * m : 4 * m + 4]
-                return
-            held[n][b] = acc.astype(BF)
-            dims = dims.replace(axis, "")
-        axis = order[n]
-        going[b] = [
-            rdma(b, 3 * n + d, held[n].at[(b, *pick(dims, axis, step(position[axis], d)))], got[n].at[b, d - 1], along[axis][d - 1])
-            for d in (1, 2, 3)
-        ]
+            acc = t1[b, position[p], position[q]].astype(F32)
+            for m in range(15):
+                acc = acc + r2[b, m].astype(F32)
+            out, first = (qg_ref, 512 * b) if b < 3 else (og_ref, 0)
+            for m in range(4):
+                out[:, first + 128 * m : first + 128 * m + 128] = acc[4 * m : 4 * m + 4]
 
     project(0, 3)
     send(1)
+    project_grad(0, 3)
     attend(0, 3)
+    attend_back(0, 3)
+
     halo_arrived(0)
     project(3, 5)
     attend(3, 5)
+    halo_arrived(1)
+    project_grad(3, 5)
+    term(3)
     finish_out(3, 5)
     send_back(0)
-    halo_arrived(1)
-    for w in range(NW):
-        gw[w * T : w * T + T] = wide[1, w].astype(BF)
-    term(3)
-    finish_out(0, 3)
-    for n in range(2):
-        do_s[n] = nn(gw[...], wot_s[:, 256 * n : 256 * n + 256]).astype(BF)
-    attend_back(3, 1)
+    attend_back(3, 2)
     stage(3, 0)
-    attend_back(4, 4)
+    attend_back(5, 3)
     finish_grad(3, 5)
     send_back(1)
-    stage(3, 1)
-    attend_back(0, 3)
+
     term(0)
     term(1)
     stage(0, 0)
     term(2)
     stage(1, 0)
-    stage(3, 2)
+    stage(2, 0)
+    stage(3, 1)
     finish_grad(0, 3)
-    stage(2, 0)
+    finish_out(0, 3)
 
     def assemble(which, dst):
         for copy in halo_out[which]:
@@ -387,13 +404,12 @@
                 dst[l, a] = rows_s[at_].astype(BF)
 
     assemble(0, of_ref)
-    for n in (1, 2):
-        for b in range(3):
-            stage(b, n)
-        if n == 1:
-            assemble(1, df_ref)
-    for b in range(4):
-        stage(b, 3)
+    for b in range(3):
+        stage(b, 1)
+    stage(3, 2)
+    assemble(1, df_ref)
+    for b in range(3):
+        stage(b, 2)
 
 
 def shards(fields, cotangent, qkv_weight, out_weight):
@@ -435,12 +451,10 @@
                 pltpu.VMEM((4, 4, 4, 4, 16, 128), BF),
                 pltpu.VMEM((4, 3, 4, 4, 16, 128), BF),
                 pltpu.VMEM((4, 4, 4, 16, 128), BF),
-                pltpu.VMEM((4, 3, 4, 16, 128), BF),
-                pltpu.VMEM((4, 4, 16, 128), BF),
-                pltpu.VMEM((4, 3, 16, 128), BF),
+                pltpu.VMEM((4, 15, 16, 128), BF),
                 pltpu.VMEM((4, 4, 4, 16, 128), F32),
-                pltpu.SemaphoreType.DMA((4, 10)),
-                pltpu.SemaphoreType.DMA((4, 10)),
+                pltpu.SemaphoreType.DMA((4, 19)),
+                pltpu.SemaphoreType.DMA((4, 19)),
             ],
             compiler_params=pltpu.CompilerParams(
                 collective_id=0, has_side_effects=True, vmem_limit_bytes=58 * 1024 * 1024

time: 60.1 us -> 56.5 us (0.940)
  Pallas kernels: 59.1 us -> 55.3 us
    pallas_call x1, Pallas kernels: 57.7 us -> 53.9 us  [shards(): pl.pallas_call(kernel, out_shape=[pltpu.VMEM((2, 24, 24, D), BF), pltpu.V...]
where the time goes in v3:
time: 56.5 us; the launch traced here: 56.1 us
  Pallas kernels  55.3 us (98%)
  between operations  0.8 us (1%)
    pallas_call x1, Pallas kernels, shards(): pl.pallas_call(kernel, out_shape=[pltpu.VMEM((2, 24, 24, D), BF), pltpu.V...  53.9 us
    pallas_call x1, Pallas kernels, shards(): pl.pallas_call(hand_over, out_shape=[jax.ShapeDtypeStruct(r.shape, r.dtyp...  1.44 us

profile of v3, /device:TPU:0, one launch (start us, length us, event | category | flops | bytes accessed | tf_op | source)
XLA Modules:
  0.0 56.1 jit_solution(11511076637094762014)
XLA Ops:
  0.6 53.9 %shard_map.75 = (bf16[2,24,24,512]{3,2,1,0:T(8,128)(2,1)S(1)}, bf16[2,24,24,512]{3,2,1,0:T(8,128)(2,1)S(1)}, f32[4,1536]{1,0:T(4,128)S(1)}, f32[4,512]{1,0:T(4,128)S(1)}) custom-call(bf16[2,24,24,512]{3,2,1,0:T(8,128)(2,1)} %f_any.1, bf16[2,24,24,512]{3,2,1,0:T(8,128)(2,1)} %c_any.1, bf16[512,1536]{1,0:T(8,128)(2,1)} %w_any.1, bf16[512,512]{1,0:T(8,128)(2,1)} %wo_any.1), custom_call_target="tpu_custom_call" | custom-call | flops 10000000000 | bytes 8000000 | tf_op jit(solution)/shard_map/pallas_call | solution.py:418
  54.5 1.4 %shard_map.76 = (bf16[2,24,24,512]{3,2,1,0:T(8,128)(2,1)}, bf16[2,24,24,512]{3,2,1,0:T(8,128)(2,1)}, f32[4,1536]{1,0:T(4,128)}, f32[4,512]{1,0:T(4,128)}) custom-call(bf16[2,24,24,512]{3,2,1,0:T(8,128)(2,1)S(1)} %get-tuple-element.8.refs_0_, bf16[2,24,24,512]{3,2,1,0:T(8,128)(2,1)S(1)} %get-tuple-element.9.refs_1_, f32[4,1536]{1,0:T(4,128)S(1)} %get-tuple-element.10.refs_2_, ...), custom_call_target="tpu_custom_call" | custom-call | tf_op jit(solution)/shard_map/pallas_call | solution.py:474

commit v4 on v3

--- a/solution.py
+++ b/solution.py
@@ -64,24 +64,28 @@
 
 
 def attention(w, big, q_s, k_s, v_s, p_s, o_s):
-    rows = pl.ds(pl.multiple_of(w * T, 16), T)
+    rows = slice(w * T, w * T + T)
     half = T // 2
-    query = lax.broadcasted_iota(jnp.int32, (1, 8 * T), 1) % T
-    pen0 = jnp.where(query >= half, big, 0.0)
-    pen1 = jnp.where(query < half, big, 0.0)
+    if big is not None:
+        query = lax.broadcasted_iota(jnp.int32, (1, 8 * T), 1) % T
+        pen0 = jnp.where(query >= half, big, 0.0)
+        pen1 = jnp.where(query < half, big, 0.0)
     for g in range(2):
         st = nt(k_s[g, rows, :], heads_apart(q_s[g, rows, :]))
-        top = jnp.maximum(
-            jnp.max(st[:half], axis=0, keepdims=True) - pen0, jnp.max(st[half:], axis=0, keepdims=True) - pen1
-        )
-        e = jnp.concatenate([jnp.exp2(st[:half] - (top + pen0)), jnp.exp2(st[half:] - (top + pen1))], axis=0)
+        if big is None:
+            e = jnp.exp2(st - jnp.max(st, axis=0, keepdims=True))
+        else:
+            top = jnp.maximum(
+                jnp.max(st[:half], axis=0, keepdims=True) - pen0, jnp.max(st[half:], axis=0, keepdims=True) - pen1
+            )
+            e = jnp.concatenate([jnp.exp2(st[:half] - (top + pen0)), jnp.exp2(st[half:] - (top + pen1))], axis=0)
         pb = (e * (1.0 / jnp.sum(e, axis=0, keepdims=True))).astype(BF)
         p_s[w, g] = pb
         o_s[rows, 256 * g : 256 * g + 256] = heads_together(tn(pb, v_s[g, rows, :])).astype(BF)
 
 
 def attention_back(w, q_s, k_s, v_s, p_s, do_s, dp_s):
-    rows = pl.ds(pl.multiple_of(w * T, 16), T)
+    rows = slice(w * T, w * T + T)
     for g in range(2):
         kg = k_s[g, rows, :]
         qm = heads_apart(q_s[g, rows, :])
@@ -233,12 +237,8 @@
     last = jnp.where(lat == lax.axis_size("lat") - 1, 1e9, 0.0)
 
     def attend(first, count):
-        def window(w, _):
-            big = jnp.where(w >= NW - 2, last, 0.0).astype(F32)
-            attention(w, big, q_s, k_s, v_s, p_s, o_s)
-            return 0
-
-        lax.fori_loop(first, first + count, window, 0)
+        for w in range(first, first + count):
+            attention(w, last if w >= NW - 2 else None, q_s, k_s, v_s, p_s, o_s)
 
     def project_grad(first, count):
         rows = slice(first * T, (first + count) * T)
@@ -248,11 +248,8 @@
             do_s[n, rows] = nn(gw[rows], wot_s[:, 256 * n : 256 * n + 256]).astype(BF)
 
     def attend_back(first, count):
-        def window(w, _):
+        for w in range(first, first + count):
             attention_back(w, q_s, k_s, v_s, p_s, do_s, dp_s)
-            return 0
-
-        lax.fori_loop(first, first + count, window, 0)
 
     def finish_out(first, count):
         for w in range(first, first + count):
@@ -367,9 +364,8 @@
     term(3)
     finish_out(3, 5)
     send_back(0)
-    attend_back(3, 2)
     stage(3, 0)
-    attend_back(5, 3)
+    attend_back(3, 5)
     finish_grad(3, 5)
     send_back(1)
 

time: 56.5 us -> 52.5 us (0.929)
  Pallas kernels: 55.3 us -> 51.6 us
    pallas_call x1, Pallas kernels: 53.9 us -> 50.1 us  [shards(): pl.pallas_call(kernel, out_shape=[pltpu.VMEM((2, 24, 24, D), BF), pltpu.V...]
where the time goes in v4:
time: 52.5 us; the launch traced here: 52.4 us
  Pallas kernels  51.6 us (98%)
  between operations  0.8 us (2%)
    pallas_call x1, Pallas kernels, shards(): pl.pallas_call(kernel, out_shape=[pltpu.VMEM((2, 24, 24, D), BF), pltpu.V...  50.1 us
    pallas_call x1, Pallas kernels, shards(): pl.pallas_call(hand_over, out_shape=[jax.ShapeDtypeStruct(r.shape, r.dtyp...  1.44 us

profile of v4, /device:TPU:0, one launch (start us, length us, event | category | flops | bytes accessed | tf_op | source)
XLA Modules:
  0.0 52.4 jit_solution(4299496399792884949)
XLA Ops:
  0.6 50.1 %shard_map.75 = (bf16[2,24,24,512]{3,2,1,0:T(8,128)(2,1)S(1)}, bf16[2,24,24,512]{3,2,1,0:T(8,128)(2,1)S(1)}, f32[4,1536]{1,0:T(4,128)S(1)}, f32[4,512]{1,0:T(4,128)S(1)}) custom-call(bf16[2,24,24,512]{3,2,1,0:T(8,128)(2,1)} %f_any.1, bf16[2,24,24,512]{3,2,1,0:T(8,128)(2,1)} %c_any.1, bf16[512,1536]{1,0:T(8,128)(2,1)} %w_any.1, bf16[512,512]{1,0:T(8,128)(2,1)} %wo_any.1), custom_call_target="tpu_custom_call" | custom-call | flops 10000000000 | bytes 8000000 | tf_op jit(solution)/shard_map/pallas_call | solution.py:414
  50.7 1.4 %shard_map.76 = (bf16[2,24,24,512]{3,2,1,0:T(8,128)(2,1)}, bf16[2,24,24,512]{3,2,1,0:T(8,128)(2,1)}, f32[4,1536]{1,0:T(4,128)}, f32[4,512]{1,0:T(4,128)}) custom-call(bf16[2,24,24,512]{3,2,1,0:T(8,128)(2,1)S(1)} %get-tuple-element.8.refs_0_, bf16[2,24,24,512]{3,2,1,0:T(8,128)(2,1)S(1)} %get-tuple-element.9.refs_1_, f32[4,1536]{1,0:T(4,128)S(1)} %get-tuple-element.10.refs_2_, ...), custom_call_target="tpu_custom_call" | custom-call | tf_op jit(solution)/shard_map/pallas_call | solution.py:470

commit v5 on v4

--- a/solution.py
+++ b/solution.py
@@ -210,14 +210,14 @@
 
     pack_in(0, f_ref)
     own(0, f_ref)
+    loads[2].wait()
+    loads[3].wait()
+    wt_s[...] = w_ref[...].T
+    wot_s[...] = wo_ref[...].T
     pl.semaphore_wait(barrier, len(peers))
     send(0)
     pack_in(1, c_ref)
     own(1, c_ref)
-    loads[2].wait()
-    loads[3].wait()
-    wt_s[...] = w_ref[...].T
-    wot_s[...] = wo_ref[...].T
 
     def project(first, count):
         rows = slice(first * T, (first + count) * T)
@@ -291,7 +291,7 @@
         for copy in halo_out[-1]:
             copy.start()
 
-    axes = ("x", "z", "y", "x")
+    axes = ("y", "z", "x", "x")
     going = [None] * 4
 
     def rdma(b, n, src, dst, peer):

time: 52.5 us -> 52.3 us (level)
  no operation moved by 1% of the time
where the time goes in v5:
time: 52.3 us; the launch traced here: 52.2 us
  Pallas kernels  51.4 us (98%)
  between operations  0.82 us (2%)
    pallas_call x1, Pallas kernels, shards(): pl.pallas_call(kernel, out_shape=[pltpu.VMEM((2, 24, 24, D), BF), pltpu.V...  50 us
    pallas_call x1, Pallas kernels, shards(): pl.pallas_call(hand_over, out_shape=[jax.ShapeDtypeStruct(r.shape, r.dtyp...  1.44 us

profile of v5, /device:TPU:0, one launch (start us, length us, event | category | flops | bytes accessed | tf_op | source)
XLA Modules:
  0.0 52.2 jit_solution(7378098937146364707)
XLA Ops:
  0.6 50.0 %shard_map.75 = (bf16[2,24,24,512]{3,2,1,0:T(8,128)(2,1)S(1)}, bf16[2,24,24,512]{3,2,1,0:T(8,128)(2,1)S(1)}, f32[4,1536]{1,0:T(4,128)S(1)}, f32[4,512]{1,0:T(4,128)S(1)}) custom-call(bf16[2,24,24,512]{3,2,1,0:T(8,128)(2,1)} %f_any.1, bf16[2,24,24,512]{3,2,1,0:T(8,128)(2,1)} %c_any.1, bf16[512,1536]{1,0:T(8,128)(2,1)} %w_any.1, bf16[512,512]{1,0:T(8,128)(2,1)} %wo_any.1), custom_call_target="tpu_custom_call" | custom-call | flops 10000000000 | bytes 8000000 | tf_op jit(solution)/shard_map/pallas_call | solution.py:414
  50.6 1.4 %shard_map.76 = (bf16[2,24,24,512]{3,2,1,0:T(8,128)(2,1)}, bf16[2,24,24,512]{3,2,1,0:T(8,128)(2,1)}, f32[4,1536]{1,0:T(4,128)}, f32[4,512]{1,0:T(4,128)}) custom-call(bf16[2,24,24,512]{3,2,1,0:T(8,128)(2,1)S(1)} %get-tuple-element.8.refs_0_, bf16[2,24,24,512]{3,2,1,0:T(8,128)(2,1)S(1)} %get-tuple-element.9.refs_1_, f32[4,1536]{1,0:T(4,128)S(1)} %get-tuple-element.10.refs_2_, ...), custom_call_target="tpu_custom_call" | custom-call | tf_op jit(solution)/shard_map/pallas_call | solution.py:470
